TPU v7x, 32 devices: a whole 2x2x4 slice. The times are simulated.
32 devices in a mesh: dp: 2 (over x), cent: 16 (over z, y, core).
Axes of the slice: x: 2, y: 2, z: 4, core: 2. Of those that a mesh axis runs over, the one named last changes fastest.
Arguments:
- points: bfloat16 [1536, 1024], P(('dp', 'cent')), may hold values from -6 to 6
- assign: int32 [1536], P(('dp', 'cent')), may hold values from 0 to 8191, as said below
- centroids: float32 [8192, 1024], P('cent'), may hold values from -6 to 6
- counts: int32 [8192], P('cent'), may hold values from 1 to 4
Outputs:
- new_centroids: float32 [8192, 1024], P('cent')
- best: float32 [1536], P(('dp', 'cent'))
Inputs may be any that keep to these rules, and one draw needn't show every extreme that they name: `assign`: split the points into aligned blocks of 768 points in order (the points of one dp index). In every block, the clusters k * 512 to (k + 1) * 512 - 1 receive exactly 48 points together, for every k.
All inputs are finite; a program needn't handle non-finite values.
Results may differ from a plain program's by a relative error of at most 0.0003.
Values may be sent and summed in bfloat16 or wider, within the bound.
A program may use at most 128 MiB of HBM per device.

v0:
```python
import jax
import jax.numpy as jnp
from jax import lax
from jax.sharding import PartitionSpec as P


def renorm(merged):
    return merged * lax.rsqrt(jnp.mean(merged * merged, axis=1, keepdims=True) + 1e-05)


def cluster_terms(rows, labels, kdev):
    first = lax.axis_index("cent") * kdev
    local = labels - first
    onehot = (local[None, :] == jnp.arange(kdev, dtype=jnp.int32)[:, None]).astype(jnp.bfloat16)
    return jnp.dot(onehot, rows, preferred_element_type=jnp.float32)


def per_device(points, assign, centroids, counts):
    kdev = centroids.shape[0]
    pdev = points.shape[0]
    weighted = centroids * counts.astype(jnp.float32)[:, None]
    rows, labels = (
        lax.all_gather(points, "cent", axis=0, tiled=True),
        lax.all_gather(assign, "cent", axis=0, tiled=True),
    )
    sums = cluster_terms(rows, labels, kdev)
    total = lax.psum(sums, "dp")
    fresh = renorm(weighted + total)
    rounded = fresh.astype(jnp.bfloat16)
    scores = jnp.dot(rows, rounded.T, preferred_element_type=jnp.float32)
    local_best = jnp.max(scores, axis=1)
    merged_best = lax.pmax(local_best, "cent")
    top = lax.dynamic_slice_in_dim(merged_best, lax.axis_index("cent") * pdev, pdev, 0)
    values = points.astype(jnp.float32)
    width = points.shape[1]
    scale = width * jnp.sqrt(jnp.mean(values * values, axis=1) + 1e-06)
    return (fresh, top / scale)


def solution(mesh):
    placed = (P(("dp", "cent"), None), P(("dp", "cent")), P("cent", None), P("cent"))
    return jax.shard_map(
        per_device,
        mesh=mesh,
        in_specs=placed,
        out_specs=(P("cent", None), P(("dp", "cent"))),
        check_vma=False,
    )
```

profile of v0, /device:TPU:0, one launch (start us, length us, event | category | flops | bytes accessed | tf_op | source)
XLA Modules:
  0.0 164.0 jit_solution(14195915273670389828)
XLA Ops:
  7.2 0.0 all-gather.2.cloned.1.call-start
  7.2 0.7 all-gather.2.cloned.1.call-update
  7.9 0.0 all-reduce.3.cloned.1.call-start
  7.9 1.2 dynamic-slice
  9.9 0.9 dynamic-update-slice
  10.7 13.7 %all-reduce = s32[768]{0:T(1024)S(1)} all-reduce(s32[768]{0:T(1024)S(1)} %dynamic-update-slice), channel_id=1, replica_groups=mesh['dp'=2,'cent'=16] {'cent'}, use_global_device_ids=true, to_apply=%add | all-reduce | flops 768 | bytes 6144
  24.5 28.2 %all-gather.2.cloned.1.call-done = bf16[768,1024]{1,0:T(8,128)(2,1)} async-done(((bf16[48,1024]{1,0:T(8,128)(2,1)}), bf16[768,1024]{1,0:T(8,128)(2,1)}) %all-gather.2.cloned.1.call-update) | async-done | bytes 1572880 | tf_op jit(solution)/shard_map/all_gather | solution.py:23
  52.7 0.0 copy-start.3
  52.7 3.7 %fusion = f32[512,1024]{1,0:T(8,128)} fusion(bf16[768,1024]{1,0:T(8,128)(2,1)} %all-gather.2.cloned.1.call-done, s32[768]{0:T(1024)S(1)} %broadcast_subtract_fusion), kind=kOutput, calls=%fused_computation.3 | convolution fusion | flops 805699584 | bytes 3673088 | tf_op jit(solution)/shard_map/dot_general | solution.py:15
  56.4 0.0 all-reduce.3.cloned.1.call-update
  56.5 0.7 copy-done.4
  57.1 0.0 copy-done.3
  57.1 0.1 multiply_reduce_fusion.1
  57.2 61.2 %all-reduce.3.cloned.1.call-done = f32[512,1024]{1,0:T(8,128)} async-done(((f32[512,1024]{1,0:T(8,128)}), f32[512,1024]{1,0:T(8,128)}) %all-reduce.3.cloned.1.call-update) | async-done | bytes 2097168 | tf_op jit(solution)/shard_map/psum | solution.py:27
  118.4 0.0 copy-done
  118.4 2.2 %multiply_reduce_fusion = f32[512]{0:T(512)S(1)} fusion(f32[512,1024]{1,0:T(8,128)} %all-reduce.3.cloned.1.call-done, f32[512,1024]{1,0:T(8,128)S(1)} %copy-done, f32[512]{0:T(512)S(1)} %convert_element_type.10), kind=kLoop, calls=%fused_computation | loop fusion | flops 2096640 | bytes 4198400 | tf_op jit(solution)/shard_map/reduce_sum | solution.py:8
  120.6 0.1 copy-done.1
  120.7 0.4 broadcast_multiply_fusion
  121.0 0.0 copy-start.2
  121.0 1.3 copy-done.2
  122.4 0.0 copy-done.5
  122.4 1.0 convolution_reduce_fusion
  123.4 33.2 %pmax.7 = f32[768]{0:T(1024)S(1)} all-reduce(f32[768]{0:T(1024)S(1)} %convolution_reduce_fusion), channel_id=1, replica_groups=mesh['dp'=2,'cent'=16] {'cent'}, use_global_device_ids=true, to_apply=%region_3.0 | all-reduce | flops 768 | bytes 6144 | tf_op jit(solution)/shard_map/pmax | solution.py:32
  156.6 0.6 multiply_divide_fusion
  (8 shorter events, 0.0 us)
Async XLA Ops:
  7.2 45.5 %all-gather.2.cloned.1.call-start = ((), (), s32[]{:S(2)}) async-start(), calls=%async_computation | async-start | bytes 1671168 | tf_op jit(solution)/shard_map/all_gather | solution.py:23
  7.9 110.5 %all-reduce.3.cloned.1.call-start = ((), (), s32[]{:S(2)}) async-start(), calls=%async_computation.1 | async-start | bytes 4194304 | tf_op jit(solution)/shard_map/psum | solution.py:27
  52.7 4.4 %copy-start.3 = (bf16[48,1024]{1,0:T(8,128)(2,1)S(1)}, bf16[48,1024]{1,0:T(8,128)(2,1)}, u32[]{:S(2)}) copy-start(bf16[48,1024]{1,0:T(8,128)(2,1)} %param.4) | copy-start | bytes 294916
  56.4 0.7 copy-start.4
  56.4 62.0 %copy-start = (f32[512,1024]{1,0:T(8,128)S(1)}, f32[512,1024]{1,0:T(8,128)}, u32[]{:S(2)}) copy-start(f32[512,1024]{1,0:T(8,128)} %param.6) | copy-start | bytes 6291460
  118.4 2.2 %copy-start.1 = (f32[512,1024]{1,0:T(8,128)S(1)}, f32[512,1024]{1,0:T(8,128)}, u32[]{:S(2)}) copy-start(f32[512,1024]{1,0:T(8,128)} %all-reduce.3.cloned.1.call-done) | copy-start | bytes 6291460
  120.7 1.7 %copy-start.5 = (bf16[768,1024]{1,0:T(8,128)(2,1)S(1)}, bf16[768,1024]{1,0:T(8,128)(2,1)}, u32[]{:S(2)}) copy-start(bf16[768,1024]{1,0:T(8,128)(2,1)} %all-gather.2.cloned.1.call-done) | copy-start | bytes 4718596
  121.0 1.3 copy-start.2
Sparse Core Ops, SparseCore 0:
  10.3 42.3 all-gather.1
  56.6 61.8 all-reduce.2
where the time goes:
time: 164 us
  waiting for transfers between devices  90.1 us (55%)
  blocking collectives  46.9 us (29%)
  between operations  14.7 us (9%)
  matrix products  4.77 us (3%)
  local copies, waits for them, and re-layouts  4.14 us (3%)
  other arithmetic  3.25 us (2%)
    psum x1, waiting for transfers between devices, per_device(): total = lax.psum(sums, 'dp')  61.2 us
    pmax x1, blocking collectives, per_device(): merged_best = lax.pmax(local_best, 'cent')  33.2 us
    all_gather x1, waiting for transfers between devices, per_device(): lax.all_gather(points, 'cent', axis=0, tiled=True)  28.2 us
    unnamed x1, blocking collectives  13.7 us
    unnamed x15, local copies, waits for them, and re-layouts  4.14 us
    dot_general x1, matrix products, cluster_terms(): return jnp.dot(onehot, rows, preferred_element_type=jnp.float32)  3.74 us
  transfers between devices with their start and end apart: 2, of which 2 were waited for; matrix products, arithmetic and copies ran while one was open for 1% of the time, Pallas kernels for 0%

commit v1 on v0

v1 whole, which is shorter than its diff:
```python
import functools

import jax
import jax.numpy as jnp
from jax import lax
from jax.experimental import pallas as pl
from jax.experimental.pallas import tpu as pltpu
from jax.sharding import PartitionSpec as P

F32 = jnp.float32
BF16 = jnp.bfloat16
LANES = 128
CHUNK = 128


def dot_nt(a, b):
    return lax.dot_general(a, b, (((1,), (1,)), ((), ())), preferred_element_type=F32)


def iota(shape, dim):
    return lax.broadcasted_iota(jnp.int32, shape, dim)


def remote(src, dst, send, recv, where):
    return pltpu.make_async_remote_copy(
        src_ref=src, dst_ref=dst, send_sem=send, recv_sem=recv,
        device_id=where, device_id_type=pl.DeviceIdType.MESH)


def kernel(ndp, ncent, wa, points_ref, assign_ref, cent_ref, counts_ref,
           fresh_ref, best_ref,
           pts, labs, keys, acc, sel, sellab, merged, rounded, outbest, inbest,
           pts_send, pts_recv, lab_send, lab_recv, sel_send, sel_recv,
           sl_send, sl_recv, best_send, best_recv, loc):
    pdev, width = points_ref.shape
    kdev = cent_ref.shape[0]
    wide = sellab.shape[2]
    wb = ncent // (2 * wa)
    me = lax.axis_index("cent")
    mydp = lax.axis_index("dp")
    core = lax.rem(me, 2)
    b = lax.rem(me // 2, wb)
    a = me // (2 * wb)

    fetch = pltpu.make_async_copy(cent_ref, merged, loc.at[0])
    fetch.start()

    def block(s):
        return pts.at[pl.ds(pl.multiple_of(s * pdev, 16), pdev), :]

    own = pltpu.make_async_copy(points_ref, block(me), loc.at[1])
    own.start()

    barrier = pltpu.get_barrier_semaphore()
    for o in range(1, ncent):
        pl.semaphore_signal(barrier, inc=1, device_id={"cent": lax.rem(me + o, ncent)},
                            device_id_type=pl.DeviceIdType.MESH)
    for o in range(1, ndp):
        pl.semaphore_signal(barrier, inc=1, device_id={"dp": lax.rem(mydp + o, ndp)},
                            device_id_type=pl.DeviceIdType.MESH)
    labs[me] = jnp.full((1, LANES), -1, jnp.int32)
    labs[me, 0:1, 0:pdev] = assign_ref[...]
    own.wait()
    pl.semaphore_wait(barrier, ncent + ndp - 2)

    def index(a_, b_, c_):
        return (a_ * wb + b_) * 2 + c_

    if wa == 4:
        others = [a + 1 - 2 * lax.rem(a, 2), lax.rem(a + 2, 4), 3 - a]
    else:
        others = [lax.rem(a + o, wa) for o in range(1, wa)]
    bothers = [lax.rem(b + o, wb) for o in range(1, wb)]
    sent = []

    def send(s, to):
        i = len(sent)
        c = remote(block(s), block(s), pts_send.at[i], pts_recv.at[s], {"cent": to})
        c.start()
        sent.append(c)

    def arrive(s):
        remote(block(s), block(s), pts_send.at[0], pts_recv.at[s], {"cent": me}).wait_recv()

    for b_ in bothers:
        send(me, index(a, b_, core))
    for a_ in others:
        send(me, index(a_, b, core))
    send(me, index(a, b, 1 - core))
    labcopies = []
    for o in range(1, ncent):
        to = lax.rem(me + o, ncent)
        c = remote(labs.at[me], labs.at[me], lab_send.at[o], lab_recv.at[me], {"cent": to})
        c.start()
        labcopies.append(c)

    eye = iota((CHUNK, CHUNK), 0) == iota((CHUNK, CHUNK), 1)
    fetch.wait()
    for j in range(kdev // CHUNK):
        rows = pl.ds(j * CHUNK, CHUNK)
        line = counts_ref[:, j * CHUNK:(j + 1) * CHUNK].astype(F32)
        column = jnp.sum(jnp.where(eye, line, 0.0), axis=1, keepdims=True)
        merged[rows, :] = merged[rows, :] * column

    def forward(s):
        arrive(s)
        for b_ in bothers:
            send(s, index(a, b_, core))
        send(s, index(a, b, 1 - core))

    forward(index(others[0], b, core))

    for o in range(1, ncent):
        s = lax.rem(me + o, ncent)
        remote(labs.at[s], labs.at[s], lab_send.at[0], lab_recv.at[s], {"cent": me}).wait_recv()
    local = labs[...].reshape(ncent, LANES) - me * kdev
    mine = (local >= 0) & (local < kdev) & (iota((ncent, LANES), 1) < pdev)
    ones = jnp.where(mine, 1.0, 0.0).astype(BF16)
    upper = jnp.where(iota((LANES, LANES), 0) < iota((LANES, LANES), 1), 1.0, 0.0).astype(BF16)
    lower = jnp.where(iota((ncent, ncent), 1) < iota((ncent, ncent), 0), 1.0, 0.0).astype(BF16)
    within = jnp.dot(ones, upper, preferred_element_type=F32)
    before = jnp.sum(jnp.dot(lower, ones, preferred_element_type=F32), axis=1, keepdims=True)
    keys[...] = jnp.where(mine, within + before, -1.0)

    slot = iota((pdev, LANES), 0).astype(F32)
    localf = jnp.where(mine, local + 1, 0).astype(F32)
    keyv = keys[...]
    total = jnp.zeros((pdev, LANES), F32)
    for s in range(ncent):
        total += jnp.where(slot == keyv[s:s + 1, :], localf[s:s + 1, :], 0.0)
    labcol = jnp.sum(total, axis=1, keepdims=True)
    place = iota((pdev, wide), 1) == iota((pdev, wide), 0) + mydp * pdev
    sellab[mydp] = jnp.sum(jnp.where(place, labcol, 0.0), axis=0, keepdims=True)
    slcopies = []
    for o in range(1, ndp):
        to = lax.rem(mydp + o, ndp)
        c = remote(sellab.at[mydp], sellab.at[mydp], sl_send.at[o], sl_recv.at[mydp], {"dp": to})
        c.start()
        slcopies.append(c)
    if sel.shape[0] > ndp * pdev:
        sel[ndp * pdev:, :] = jnp.zeros((sel.shape[0] - ndp * pdev, width), BF16)

    for a_ in others[1:]:
        forward(index(a_, b, core))

    def pick(s):
        key = keys[pl.ds(s, 1), :]
        choose = jnp.where(slot == key, 1.0, 0.0).astype(BF16)[:, :pdev]
        return jnp.dot(choose, block(s)[...], preferred_element_type=F32)

    acc[...] = pick(me)
    for a_ in others:
        acc[...] += pick(index(a_, b, core))
    arrive(index(a, b, 1 - core))
    acc[...] += pick(index(a, b, 1 - core))
    for a_ in others:
        s = index(a_, b, 1 - core)
        arrive(s)
        acc[...] += pick(s)
    for a_ in [a] + others:
        for b_ in bothers:
            s = index(a_, b_, core)
            arrive(s)
            send(s, index(a, b, 1 - core))
            acc[...] += pick(s)
    for a_ in [a] + others:
        for b_ in bothers:
            s = index(a_, b_, 1 - core)
            arrive(s)
            acc[...] += pick(s)

    def selrows(d):
        return sel.at[pl.ds(pl.multiple_of(d * pdev, 16), pdev), :]

    selrows(mydp)[...] = acc[...].astype(BF16)
    selcopies = []
    for o in range(1, ndp):
        to = lax.rem(mydp + o, ndp)
        c = remote(selrows(mydp), selrows(mydp), sel_send.at[o], sel_recv.at[mydp], {"dp": to})
        c.start()
        selcopies.append(c)
    for o in range(1, ndp):
        d = lax.rem(mydp + o, ndp)
        remote(sellab.at[d], sellab.at[d], sl_send.at[0], sl_recv.at[d], {"dp": mydp}).wait_recv()
        remote(selrows(d), selrows(d), sel_send.at[0], sel_recv.at[d], {"dp": mydp}).wait_recv()

    labrow = jnp.sum(sellab[...].reshape(ndp, wide), axis=0, keepdims=True) - 1.0
    outs = []
    for j in range(kdev // CHUNK):
        rows = pl.ds(j * CHUNK, CHUNK)
        ids = (iota((CHUNK, wide), 0) + j * CHUNK).astype(F32)
        onehot = jnp.where(ids == labrow, 1.0, 0.0).astype(BF16)
        value = merged[rows, :] + jnp.dot(onehot, sel[...], preferred_element_type=F32)
        value = value * lax.rsqrt(jnp.mean(value * value, axis=1, keepdims=True) + 1e-05)
        merged[rows, :] = value
        c = pltpu.make_async_copy(merged.at[rows, :], fresh_ref.at[rows, :], loc.at[2 + j])
        c.start()
        outs.append(c)
        rounded[rows, :] = value.astype(BF16)

    npts = ncent * pdev
    step = 256 if npts % 256 == 0 else 128
    parts = []
    for t in range(npts // step):
        scores = dot_nt(rounded[...], pts[t * step:(t + 1) * step, :])
        parts.append(jnp.max(scores, axis=0, keepdims=True))
    line = jnp.concatenate(parts, axis=1)
    for s in range(ncent):
        turned = pltpu.roll(line, (npts - s * pdev) % npts, 1) if s else line
        outbest[s] = turned[:, :LANES]
    bestcopies = []
    for o in range(1, ncent):
        to = lax.rem(me + o, ncent)
        c = remote(outbest.at[to], inbest.at[me], best_send.at[o], best_recv.at[me], {"cent": to})
        c.start()
        bestcopies.append(c)
    inbest[me] = outbest[me]

    values = block(me)[...].astype(F32)
    square = jnp.mean(values * values, axis=1, keepdims=True)
    diag = iota((pdev, pdev), 0) == iota((pdev, pdev), 1)
    square = jnp.sum(jnp.where(diag, square, 0.0), axis=0, keepdims=True)
    scale = width * jnp.sqrt(square + 1e-06)

    for c in sent + labcopies + slcopies + selcopies:
        c.wait_send()
    for o in range(1, ncent):
        s = lax.rem(me + o, ncent)
        remote(outbest.at[s], inbest.at[s], best_send.at[0], best_recv.at[s], {"cent": me}).wait_recv()
    top = jnp.max(inbest[...].reshape(ncent, LANES), axis=0, keepdims=True)
    best_ref[...] = top[:, :pdev] / scale
    for c in bestcopies:
        c.wait_send()
    for c in outs:
        c.wait()


def per_device(ndp, ncent, points, assign, centroids, counts):
    kdev, width = centroids.shape
    pdev = points.shape[0]
    wa = 4
    wb = ncent // (2 * wa)
    wide = -(-ndp * pdev // LANES) * LANES
    nsend = (wa - 1) + (wb - 1) * wa + wa * wb
    vmem = pl.BlockSpec(memory_space=pltpu.VMEM)
    anyspace = pl.BlockSpec(memory_space=pl.ANY)
    dma = pltpu.SemaphoreType.DMA
    fresh, best = pl.pallas_call(
        functools.partial(kernel, ndp, ncent, wa),
        out_shape=(jax.ShapeDtypeStruct((kdev, width), F32), jax.ShapeDtypeStruct((1, pdev), F32)),
        in_specs=[anyspace, vmem, anyspace, vmem],
        out_specs=(anyspace, vmem),
        scratch_shapes=[
            pltpu.VMEM((ncent * pdev, width), BF16),
            pltpu.VMEM((ncent, 1, LANES), jnp.int32),
            pltpu.VMEM((ncent, LANES), F32),
            pltpu.VMEM((pdev, width), F32),
            pltpu.VMEM((wide, width), BF16),
            pltpu.VMEM((ndp, 1, wide), F32),
            pltpu.VMEM((kdev, width), F32),
            pltpu.VMEM((kdev, width), BF16),
            pltpu.VMEM((ncent, 1, LANES), F32),
            pltpu.VMEM((ncent, 1, LANES), F32),
            dma((nsend,)), dma((ncent,)), dma((ncent,)), dma((ncent,)),
            dma((ndp,)), dma((ndp,)), dma((ndp,)), dma((ndp,)),
            dma((ncent,)), dma((ncent,)), dma((2 + kdev // CHUNK,)),
        ],
        compiler_params=pltpu.CompilerParams(
            collective_id=0, has_side_effects=True, vmem_limit_bytes=32 * 2**20),
    )(points, assign.reshape(1, pdev), centroids, counts.reshape(1, kdev))
    return fresh, best.reshape(pdev)


def solution(mesh):
    placed = (P(("dp", "cent"), None), P(("dp", "cent")), P("cent", None), P("cent"))
    return jax.shard_map(
        functools.partial(per_device, mesh.shape["dp"], mesh.shape["cent"]),
        mesh=mesh,
        in_specs=placed,
        out_specs=(P("cent", None), P(("dp", "cent"))),
        check_vma=False,
    )
```

time: 164 us -> 42.6 us (0.26)
  waiting for transfers between devices: 90.1 us -> 0 us
  blocking collectives: 46.9 us -> 0 us
  Pallas kernels: 0 us -> 36.1 us
  between operations: 14.7 us -> 0.65 us
  matrix products: 4.77 us -> 0 us
  other arithmetic: 3.25 us -> 0 us
    psum x1 -> x0, waiting for transfers between devices: 61.2 us -> none  [per_device(): total = lax.psum(sums, 'dp')]
    pallas_call x0 -> x1, Pallas kernels: none -> 36.1 us  [per_device(): pl.pallas_call(functools.partial(kernel, ndp, ncent, wa), out_shape=(jax....]
    pmax x1 -> x0, blocking collectives: 33.2 us -> none  [per_device(): merged_best = lax.pmax(local_best, 'cent')]
    all_gather x1 -> x0, waiting for transfers between devices: 28.2 us -> none  [per_device(): lax.all_gather(points, 'cent', axis=0, tiled=True)]
    unnamed x1 -> x0, blocking collectives: 13.7 us -> none
    dot_general x2 -> x0, matrix products: 4.77 us -> none  [the longest x1 3.74 us: cluster_terms(): return jnp.dot(onehot, rows, preferred_element_type=jnp.float32)]
    reduce_sum x2 -> x0, other arithmetic: 2.28 us -> none  [the longest x1 2.16 us: renorm(): jnp.mean(merged * merged, axis=1, keepdims=True) + 1e-05]
    unnamed x15 -> x10, local copies, waits for them, and re-layouts: 4.14 us -> 5.64 us
  transfers between devices with their start and end apart: 2 -> 0, of which waited for: 2 -> 0; matrix products, arithmetic and copies ran while one was open for 1% -> 0% of each run, Pallas kernels for 0% -> 0%
where the time goes in v1:
time: 42.6 us; the launch traced here: 42.4 us
  Pallas kernels  36.1 us (85%)
  local copies, waits for them, and re-layouts  5.64 us (13%)
  between operations  0.65 us (2%)
    pallas_call x1, Pallas kernels, per_device(): pl.pallas_call(functools.partial(kernel, ndp, ncent, wa), out_shape=(jax....  36.1 us
    unnamed x10, local copies, waits for them, and re-layouts  5.64 us

profile of v1, /device:TPU:0, one launch (start us, length us, event | category | flops | bytes accessed | tf_op | source)
XLA Modules:
  0.0 42.4 jit_solution(16330216385461052263)
XLA Ops:
  0.6 0.0 copy-start
  0.6 1.6 %copy-done = f32[512,1024]{1,0:T(8,128)S(1)} copy-done((f32[512,1024]{1,0:T(8,128)S(1)}, f32[512,1024]{1,0:T(8,128)}, u32[]{:S(2)}) %copy-start) | copy-done | bytes 2097176
  2.2 0.0 copy-start.1
  2.2 0.9 %copy-done.1 = bf16[48,1024]{1,0:T(8,128)(2,1)S(1)} copy-done((bf16[48,1024]{1,0:T(8,128)(2,1)S(1)}, bf16[48,1024]{1,0:T(8,128)(2,1)}, u32[]{:S(2)}) %copy-start.1) | copy-done | bytes 98328
  3.1 0.0 copy-start.2
  3.1 0.7 %copy-done.2 = s32[512]{0:T(512)S(1)} copy-done((s32[512]{0:T(512)S(1)}, s32[512]{0:T(512)}, u32[]{:S(2)}) %copy-start.2) | copy-done | bytes 2072
  3.8 0.0 copy-start.3
  3.8 0.7 %copy-done.3 = s32[48]{0:T(128)S(1)} copy-done((s32[48]{0:T(128)S(1)}, s32[48]{0:T(128)}, u32[]{:S(2)}) %copy-start.3) | copy-done | bytes 216
  4.5 36.1 %shard_map.59 = (f32[512,1024]{1,0:T(8,128)S(1)}, f32[1,48]{1,0:T(1,128)S(1)}) custom-call(bf16[48,1024]{1,0:T(8,128)(2,1)S(1)} %copy-done.1, s32[1,48]{1,0:T(1,128)S(1)} %bitcast.4, f32[512,1024]{1,0:T(8,128)S(1)} %copy-done, s32[1,512]{1,0:T(1,128)S(1)} %bitcast.3), custom_call_target="tpu_custom_call" | custom-call | tf_op jit(solution)/shard_map/pallas_call | solution.py:248
  40.5 1.3 %copy.8 = f32[512,1024]{1,0:T(8,128)} copy(f32[512,1024]{1,0:T(8,128)S(1)} %get-tuple-element.8) | data formatting | bytes 4194304
  41.8 0.5 %copy.9 = f32[48]{0:T(128)} copy(f32[48]{0:T(128)S(1)} %bitcast.5) | data formatting | bytes 384
Async XLA Ops:
  0.6 1.6 %copy-start = (f32[512,1024]{1,0:T(8,128)S(1)}, f32[512,1024]{1,0:T(8,128)}, u32[]{:S(2)}) copy-start(f32[512,1024]{1,0:T(8,128)} %cent_ref.1) | copy-start | bytes 6291460
  2.2 0.9 %copy-start.1 = (bf16[48,1024]{1,0:T(8,128)(2,1)S(1)}, bf16[48,1024]{1,0:T(8,128)(2,1)}, u32[]{:S(2)}) copy-start(bf16[48,1024]{1,0:T(8,128)(2,1)} %points_ref.1) | copy-start | bytes 294916
  3.1 0.7 %copy-start.2 = (s32[512]{0:T(512)S(1)}, s32[512]{0:T(512)}, u32[]{:S(2)}) copy-start(s32[512]{0:T(512)} %param.7) | copy-start | bytes 6148
  3.8 0.7 %copy-start.3 = (s32[48]{0:T(128)S(1)}, s32[48]{0:T(128)}, u32[]{:S(2)}) copy-start(s32[48]{0:T(128)} %param.5) | copy-start | bytes 580

commit v2 on v1

--- a/solution.py
+++ b/solution.py
@@ -67,25 +67,32 @@
         return (a_ * wb + b_) * 2 + c_
 
     if wa == 4:
-        others = [a + 1 - 2 * lax.rem(a, 2), lax.rem(a + 2, 4), 3 - a]
+        half = a // 2
+        others = [1 - a + 4 * half, 2 - half, 3 - 3 * half]
     else:
         others = [lax.rem(a + o, wa) for o in range(1, wa)]
     bothers = [lax.rem(b + o, wb) for o in range(1, wb)]
     sent = []
 
-    def send(s, to):
+    def send(s, to, when=None):
         i = len(sent)
-        c = remote(block(s), block(s), pts_send.at[i], pts_recv.at[s], {"cent": to})
-        c.start()
-        sent.append(c)
+
+        def copy():
+            return remote(block(s), block(s), pts_send.at[i], pts_recv.at[s], {"cent": to})
+
+        sent.append((when, copy))
+        if when is None:
+            copy().start()
+        else:
+            pl.when(when)(lambda: copy().start())
 
     def arrive(s):
         remote(block(s), block(s), pts_send.at[0], pts_recv.at[s], {"cent": me}).wait_recv()
 
     for b_ in bothers:
         send(me, index(a, b_, core))
-    for a_ in others:
-        send(me, index(a_, b, core))
+    send(me, index(a - 1, b, core), a > 0)
+    send(me, index(a + 1, b, core), a < wa - 1)
     send(me, index(a, b, 1 - core))
     labcopies = []
     for o in range(1, ncent):
@@ -102,13 +109,18 @@
         column = jnp.sum(jnp.where(eye, line, 0.0), axis=1, keepdims=True)
         merged[rows, :] = merged[rows, :] * column
 
-    def forward(s):
-        arrive(s)
-        for b_ in bothers:
-            send(s, index(a, b_, core))
-        send(s, index(a, b, 1 - core))
-
-    forward(index(others[0], b, core))
+    for k in range(1, wa):
+        for way in (1, -1):
+            origin = a + way * k
+            valid = (origin < wa) if way > 0 else (origin >= 0)
+            onward = (a > 0) if way > 0 else (a < wa - 1)
+            s = index(origin, b, core)
+            pl.when(valid)(lambda s=s: arrive(s))
+            if k < wa - 1:
+                send(s, index(a - way, b, core), valid & onward)
+            for b_ in bothers:
+                send(s, index(a, b_, core), valid)
+            send(s, index(a, b, 1 - core), valid)
 
     for o in range(1, ncent):
         s = lax.rem(me + o, ncent)
@@ -139,9 +151,6 @@
         slcopies.append(c)
     if sel.shape[0] > ndp * pdev:
         sel[ndp * pdev:, :] = jnp.zeros((sel.shape[0] - ndp * pdev, width), BF16)
-
-    for a_ in others[1:]:
-        forward(index(a_, b, core))
 
     def pick(s):
         key = keys[pl.ds(s, 1), :]
@@ -185,17 +194,13 @@
         remote(selrows(d), selrows(d), sel_send.at[0], sel_recv.at[d], {"dp": mydp}).wait_recv()
 
     labrow = jnp.sum(sellab[...].reshape(ndp, wide), axis=0, keepdims=True) - 1.0
-    outs = []
     for j in range(kdev // CHUNK):
         rows = pl.ds(j * CHUNK, CHUNK)
         ids = (iota((CHUNK, wide), 0) + j * CHUNK).astype(F32)
         onehot = jnp.where(ids == labrow, 1.0, 0.0).astype(BF16)
         value = merged[rows, :] + jnp.dot(onehot, sel[...], preferred_element_type=F32)
         value = value * lax.rsqrt(jnp.mean(value * value, axis=1, keepdims=True) + 1e-05)
-        merged[rows, :] = value
-        c = pltpu.make_async_copy(merged.at[rows, :], fresh_ref.at[rows, :], loc.at[2 + j])
-        c.start()
-        outs.append(c)
+        fresh_ref[rows, :] = value
         rounded[rows, :] = value.astype(BF16)
 
     npts = ncent * pdev
@@ -222,7 +227,12 @@
     square = jnp.sum(jnp.where(diag, square, 0.0), axis=0, keepdims=True)
     scale = width * jnp.sqrt(square + 1e-06)
 
-    for c in sent + labcopies + slcopies + selcopies:
+    for when, copy in sent:
+        if when is None:
+            copy().wait_send()
+        else:
+            pl.when(when)(lambda copy=copy: copy().wait_send())
+    for c in labcopies + slcopies + selcopies:
         c.wait_send()
     for o in range(1, ncent):
         s = lax.rem(me + o, ncent)
@@ -231,8 +241,6 @@
     best_ref[...] = top[:, :pdev] / scale
     for c in bestcopies:
         c.wait_send()
-    for c in outs:
-        c.wait()
 
 
 def per_device(ndp, ncent, points, assign, centroids, counts):
@@ -241,15 +249,15 @@
     wa = 4
     wb = ncent // (2 * wa)
     wide = -(-ndp * pdev // LANES) * LANES
-    nsend = (wa - 1) + (wb - 1) * wa + wa * wb
+    nsend = wb + 2 + 2 * (wa - 1) * (wb + 1) + wa * wb
     vmem = pl.BlockSpec(memory_space=pltpu.VMEM)
-    anyspace = pl.BlockSpec(memory_space=pl.ANY)
+    hbm = pl.BlockSpec(memory_space=pltpu.MemorySpace.HBM)
     dma = pltpu.SemaphoreType.DMA
     fresh, best = pl.pallas_call(
         functools.partial(kernel, ndp, ncent, wa),
-        out_shape=(jax.ShapeDtypeStruct((kdev, width), F32), jax.ShapeDtypeStruct((1, pdev), F32)),
-        in_specs=[anyspace, vmem, anyspace, vmem],
-        out_specs=(anyspace, vmem),
+        out_shape=(pltpu.MemorySpace.VMEM((kdev, width), F32), jax.ShapeDtypeStruct((1, pdev), F32)),
+        in_specs=[hbm, vmem, hbm, vmem],
+        out_specs=(vmem, vmem),
         scratch_shapes=[
             pltpu.VMEM((ncent * pdev, width), BF16),
             pltpu.VMEM((ncent, 1, LANES), jnp.int32),
@@ -263,10 +271,10 @@
             pltpu.VMEM((ncent, 1, LANES), F32),
             dma((nsend,)), dma((ncent,)), dma((ncent,)), dma((ncent,)),
             dma((ndp,)), dma((ndp,)), dma((ndp,)), dma((ndp,)),
-            dma((ncent,)), dma((ncent,)), dma((2 + kdev // CHUNK,)),
+            dma((ncent,)), dma((ncent,)), dma((2,)),
         ],
         compiler_params=pltpu.CompilerParams(
-            collective_id=0, has_side_effects=True, vmem_limit_bytes=32 * 2**20),
+            collective_id=0, has_side_effects=True, vmem_limit_bytes=60 * 2**20),
     )(points, assign.reshape(1, pdev), centroids, counts.reshape(1, kdev))
     return fresh, best.reshape(pdev)
 

time: 42.6 us -> 36.8 us (0.86)
  local copies, waits for them, and re-layouts: 5.64 us -> 1.84 us
  Pallas kernels: 36.1 us -> 34.1 us
    unnamed x10 -> x4, local copies, waits for them, and re-layouts: 5.64 us -> 1.84 us
    pallas_call x1, Pallas kernels: 36.1 us -> 34.1 us  [per_device(): pl.pallas_call(functools.partial(kernel, ndp, ncent, wa), out_shape=(pltp...]
where the time goes in v2:
time: 36.8 us; the launch traced here: 36.6 us
  Pallas kernels  34.1 us (93%)
  local copies, waits for them, and re-layouts  1.84 us (5%)
  between operations  0.65 us (2%)
    pallas_call x1, Pallas kernels, per_device(): pl.pallas_call(functools.partial(kernel, ndp, ncent, wa), out_shape=(pltp...  34.1 us
    unnamed x4, local copies, waits for them, and re-layouts  1.84 us

profile of v2, /device:TPU:0, one launch (start us, length us, event | category | flops | bytes accessed | tf_op | source)
XLA Modules:
  0.0 36.6 jit_solution(428779510833536308)
XLA Ops:
  0.6 34.1 %shard_map.59 = (f32[512,1024]{1,0:T(8,128)S(1)}, f32[1,48]{1,0:T(1,128)}) custom-call(bf16[48,1024]{1,0:T(8,128)(2,1)} %points_ref.1, s32[1,48]{1,0:T(1,128)} %bitcast.4, f32[512,1024]{1,0:T(8,128)} %cent_ref.1, s32[1,512]{1,0:T(1,128)} %bitcast.3), custom_call_target="tpu_custom_call" | custom-call | tf_op jit(solution)/shard_map/pallas_call | solution.py:256
  34.7 0.0 copy-start
  34.8 1.3 %copy.8 = f32[512,1024]{1,0:T(8,128)} copy(f32[512,1024]{1,0:T(8,128)S(1)} %get-tuple-element.6) | data formatting | bytes 4194304
  36.1 0.0 copy-done
  36.1 0.5 %copy.9 = f32[48]{0:T(128)} copy(f32[48]{0:T(128)S(1)} %bitcast.5) | data formatting | bytes 384
Async XLA Ops:
  34.7 1.3 %copy-start = (f32[1,48]{1,0:T(1,128)S(1)}, f32[1,48]{1,0:T(1,128)}, u32[]{:S(2)}) copy-start(f32[1,48]{1,0:T(1,128)} %get-tuple-element.5) | copy-start | bytes 580

commit v3 on v2

--- a/solution.py
+++ b/solution.py
@@ -11,6 +11,7 @@
 BF16 = jnp.bfloat16
 LANES = 128
 CHUNK = 128
+PIECES = 2
 
 
 def dot_nt(a, b):
@@ -74,11 +75,17 @@
     bothers = [lax.rem(b + o, wb) for o in range(1, wb)]
     sent = []
 
-    def send(s, to, when=None):
+    piece = width // PIECES
+
+    def part(s, q):
+        rows = pl.ds(pl.multiple_of(s * pdev, 16), pdev)
+        return block(s) if q is None else pts.at[rows, q * piece:(q + 1) * piece]
+
+    def send(s, to, q, when=None):
         i = len(sent)
 
         def copy():
-            return remote(block(s), block(s), pts_send.at[i], pts_recv.at[s], {"cent": to})
+            return remote(part(s, q), part(s, q), pts_send.at[i], pts_recv.at[s, q or 0], {"cent": to})
 
         sent.append((when, copy))
         if when is None:
@@ -86,14 +93,15 @@
         else:
             pl.when(when)(lambda: copy().start())
 
-    def arrive(s):
-        remote(block(s), block(s), pts_send.at[0], pts_recv.at[s], {"cent": me}).wait_recv()
-
-    for b_ in bothers:
-        send(me, index(a, b_, core))
-    send(me, index(a - 1, b, core), a > 0)
-    send(me, index(a + 1, b, core), a < wa - 1)
-    send(me, index(a, b, 1 - core))
+    def arrive(s, q=None):
+        remote(part(s, q), part(s, q), pts_send.at[0], pts_recv.at[s, q or 0], {"cent": me}).wait_recv()
+
+    for q in range(PIECES):
+        send(me, index(a - 1, b, core), q, a > 0)
+        send(me, index(a + 1, b, core), q, a < wa - 1)
+        for b_ in bothers:
+            send(me, index(a, b_, core), q)
+    send(me, index(a, b, 1 - core), None)
     labcopies = []
     for o in range(1, ncent):
         to = lax.rem(me + o, ncent)
@@ -110,17 +118,19 @@
         merged[rows, :] = merged[rows, :] * column
 
     for k in range(1, wa):
-        for way in (1, -1):
-            origin = a + way * k
-            valid = (origin < wa) if way > 0 else (origin >= 0)
-            onward = (a > 0) if way > 0 else (a < wa - 1)
-            s = index(origin, b, core)
-            pl.when(valid)(lambda s=s: arrive(s))
-            if k < wa - 1:
-                send(s, index(a - way, b, core), valid & onward)
-            for b_ in bothers:
-                send(s, index(a, b_, core), valid)
-            send(s, index(a, b, 1 - core), valid)
+        for q in range(PIECES):
+            for way in (1, -1):
+                origin = a + way * k
+                valid = (origin < wa) if way > 0 else (origin >= 0)
+                onward = (a > 0) if way > 0 else (a < wa - 1)
+                s = index(origin, b, core)
+                pl.when(valid)(lambda s=s, q=q: arrive(s, q))
+                if k < wa - 1:
+                    send(s, index(a - way, b, core), q, valid & onward)
+                for b_ in bothers:
+                    send(s, index(a, b_, core), q, valid)
+                if q == PIECES - 1:
+                    send(s, index(a, b, 1 - core), None, valid)
 
     for o in range(1, ncent):
         s = lax.rem(me + o, ncent)
@@ -169,8 +179,9 @@
     for a_ in [a] + others:
         for b_ in bothers:
             s = index(a_, b_, core)
-            arrive(s)
-            send(s, index(a, b, 1 - core))
+            for q in range(PIECES):
+                arrive(s, q)
+            send(s, index(a, b, 1 - core), None)
             acc[...] += pick(s)
     for a_ in [a] + others:
         for b_ in bothers:
@@ -249,7 +260,7 @@
     wa = 4
     wb = ncent // (2 * wa)
     wide = -(-ndp * pdev // LANES) * LANES
-    nsend = wb + 2 + 2 * (wa - 1) * (wb + 1) + wa * wb
+    nsend = PIECES * (wb + 2 + 2 * (wa - 1) * (wb + 1)) + wa * wb
     vmem = pl.BlockSpec(memory_space=pltpu.VMEM)
     hbm = pl.BlockSpec(memory_space=pltpu.MemorySpace.HBM)
     dma = pltpu.SemaphoreType.DMA
@@ -269,7 +280,7 @@
             pltpu.VMEM((kdev, width), BF16),
             pltpu.VMEM((ncent, 1, LANES), F32),
             pltpu.VMEM((ncent, 1, LANES), F32),
-            dma((nsend,)), dma((ncent,)), dma((ncent,)), dma((ncent,)),
+            dma((nsend,)), dma((ncent, PIECES)), dma((ncent,)), dma((ncent,)),
             dma((ndp,)), dma((ndp,)), dma((ndp,)), dma((ndp,)),
             dma((ncent,)), dma((ncent,)), dma((2,)),
         ],

time: 36.8 us -> 35.5 us (0.965)
  Pallas kernels: 34.1 us -> 32.9 us
    pallas_call x1, Pallas kernels: 34.1 us -> 32.9 us  [per_device(): pl.pallas_call(functools.partial(kernel, ndp, ncent, wa), out_shape=(pltp...]
where the time goes in v3:
time: 35.5 us; the launch traced here: 35.4 us
  Pallas kernels  32.9 us (93%)
  local copies, waits for them, and re-layouts  1.84 us (5%)
  between operations  0.65 us (2%)
    pallas_call x1, Pallas kernels, per_device(): pl.pallas_call(functools.partial(kernel, ndp, ncent, wa), out_shape=(pltp...  32.9 us
    unnamed x4, local copies, waits for them, and re-layouts  1.84 us

profile of v3, /device:TPU:0, one launch (start us, length us, event | category | flops | bytes accessed | tf_op | source)
XLA Modules:
  0.0 35.4 jit_solution(17658871021599664456)
XLA Ops:
  0.6 32.9 %shard_map.59 = (f32[512,1024]{1,0:T(8,128)S(1)}, f32[1,48]{1,0:T(1,128)}) custom-call(bf16[48,1024]{1,0:T(8,128)(2,1)} %points_ref.1, s32[1,48]{1,0:T(1,128)} %bitcast.4, f32[512,1024]{1,0:T(8,128)} %cent_ref.1, s32[1,512]{1,0:T(1,128)} %bitcast.3), custom_call_target="tpu_custom_call" | custom-call | tf_op jit(solution)/shard_map/pallas_call | solution.py:267
  33.5 0.0 copy-start
  33.5 1.3 %copy.8 = f32[512,1024]{1,0:T(8,128)} copy(f32[512,1024]{1,0:T(8,128)S(1)} %get-tuple-element.6) | data formatting | bytes 4194304
  34.8 0.0 copy-done
  34.8 0.5 %copy.9 = f32[48]{0:T(128)} copy(f32[48]{0:T(128)S(1)} %bitcast.5) | data formatting | bytes 384
Async XLA Ops:
  33.5 1.3 %copy-start = (f32[1,48]{1,0:T(1,128)S(1)}, f32[1,48]{1,0:T(1,128)}, u32[]{:S(2)}) copy-start(f32[1,48]{1,0:T(1,128)} %get-tuple-element.5) | copy-start | bytes 580
